TPU v7x, 128 devices: a whole 4x4x4 slice. The times are simulated.
128 devices in a mesh: grp: 2 (over core), own: 64 (over y, z, x).
Axes of the slice: x: 4, y: 4, z: 4, core: 2. Of those that a mesh axis runs over, the one named last changes fastest.
Arguments:
- row_x: bfloat16 [131072, 1024], P(('grp', 'own')), parts along dimension 0, may hold values from -6 to 6
- row_user: int32 [131072, 1], P(('grp', 'own')), parts along dimension 0, may hold values from 0 to 63; in each aligned block of 1024 rows (0 to 1023, 1024 to 2047, ...) at most 32 rows name the same one
- user_owner: int32 [128], P('grp'), parts along dimension 0, may hold values from 0 to 63, each once
- hist_len: int32 [128], P(('grp', 'own')), parts along dimension 0, may hold values from 1 to 1024, 32768 in all
- new_rows: bfloat16 [128, 64, 1024], P(('grp', 'own')), parts along dimension 0, may hold values from -6 to 6
- cache_keys: bfloat16 [128, 1024, 1024], P(('grp', 'own')), parts along dimension 0, may hold values from -6 to 6
- cache_values: bfloat16 [128, 1024, 1024], P(('grp', 'own')), parts along dimension 0, may hold values from -6 to 6
- w_in: bfloat16 [1024, 4096], replicated, may hold values from -0.1875 to 0.1875
- w_out: bfloat16 [1024, 1024], replicated, may hold values from -0.1875 to 0.1875
- w_score: float32 [1024], replicated, may hold values from -0.1875 to 0.1875
Outputs:
- scores: float32 [131072], P(('grp', 'own')), parts along dimension 0
- new_out: bfloat16 [128, 64, 1024], P(('grp', 'own')), parts along dimension 0
There are 2 independent parts, one for each index of `grp`. A program takes and returns all parts, laid end to end along the dimension named above; an argument that names none is the same for every part. Nothing has to cross between parts.
Inputs may be any that keep to these rules, and one draw needn't show every extreme that they name: `row_user`: among the rows of one device no user appears more than 32 times, and some user appears exactly 32 times. `user_owner`: each device index appears once.
All inputs are finite; a program needn't handle non-finite values. No bound on the sum of `hist_len` on one device may be relied on, other than what follows from the above.
Results may differ from a plain program's by a relative error of at most 0.0095.
Values may be sent and summed in bfloat16 or wider, within the bound.
No kernel may reach another device: no remote copies, remote signals or barrier semaphores. Data moves between devices by JAX's collectives and lax.ppermute only.
A program may use at most 128 MiB of HBM per device.

v0:
```python
import jax
import jax.numpy as jnp
from jax import lax
from jax.experimental import pallas as pl
from jax.experimental.pallas import tpu as pltpu
from jax.sharding import PartitionSpec as P

HEADS = 8
NEW = 64
BF = jnp.bfloat16
F32 = jnp.float32
VMEM_LIMIT = 56 * 1024 * 1024
SLOTS = 16
TILE = 512


def dot(a, b, dims=((1,), (0,))):
    return lax.dot_general(a, b, (dims, ((), ())), preferred_element_type=F32)


def normalize(v):
    mean = jnp.mean(v, axis=-1, keepdims=True)
    cent = v - mean
    var = jnp.mean(cent * cent, axis=-1, keepdims=True)
    return cent * lax.rsqrt(var + 1e-06)


def silu(v):
    half = 0.5 * v
    return half + half * jnp.tanh(half)


def split3(v):
    hi = v.astype(BF)
    rest = v - hi.astype(F32)
    mid = rest.astype(BF)
    low = (rest - mid.astype(F32)).astype(BF)
    return hi, mid, low


def split_rows(row):
    width = row.shape[1]
    hi, mid, low = split3(row)
    place = lax.broadcasted_iota(jnp.int32, (8, width), 0)
    parts = jnp.where(place == 0, hi.astype(F32), 0.0)
    parts = jnp.where(place == 1, mid.astype(F32), parts)
    return jnp.where(place == 2, low.astype(F32), parts).astype(BF)


def place_rows(user_ref, owner_ref, place_ref):
    rows = user_ref.shape[1]
    users = owner_ref.shape[1]
    step = 128
    along = lax.broadcasted_iota(jnp.int32, (users, users), 0)
    across = lax.broadcasted_iota(jnp.int32, (users, users), 1)
    owners = jnp.sum(
        jnp.where(along == across, owner_ref[...], 0).astype(F32), axis=1, keepdims=True
    )
    before = lax.broadcasted_iota(jnp.int32, (step, step), 0) < lax.broadcasted_iota(
        jnp.int32, (step, step), 1
    )
    before = jnp.where(before, 1.0, 0.0).astype(BF)
    seen = jnp.zeros((users, 1), F32)
    for b in range(rows // step):
        part = slice(b * step, (b + 1) * step)
        match = lax.broadcasted_iota(jnp.int32, (users, step), 0) == user_ref[:, part]
        match = jnp.where(match, 1.0, 0.0)
        earlier = dot(match.astype(BF), before) + seen
        seen = seen + jnp.sum(match, axis=1, keepdims=True)
        position = jnp.sum(earlier * match, axis=0, keepdims=True)
        owner = jnp.sum(owners * match, axis=0, keepdims=True)
        place_ref[0:1, part] = owner.astype(jnp.int32)
        place_ref[1:2, part] = position.astype(jnp.int32)


def fill(out_ref, slots, first, place_ref, normed_ref, done=None):
    rows = normed_ref.shape[0]
    owner = place_ref[0:1, :]
    position = place_ref[1:2, :]
    inside = jnp.logical_and(position >= first, position < first + slots)
    key = jnp.where(inside, owner * slots + position - first, -1)
    step = 256
    for b in range(out_ref.shape[0] // step):
        at = lax.broadcasted_iota(jnp.int32, (step, rows), 0) + b * step
        pick = jnp.where(at == key, 1.0, 0.0).astype(BF)
        out_ref[b * step : (b + 1) * step, :] = dot(pick, normed_ref[...]).astype(BF)
        if done is not None:
            done(b, slice(b * step, (b + 1) * step))


def route_kernel(slots, x_ref, user_ref, owner_ref, buf_ref, place_ref):
    place_rows(user_ref, owner_ref, place_ref)
    fill(buf_ref, slots, 0, place_ref, x_ref)


def fill_second(slots, first, x_ref, place_ref, score_ref, buf_ref, base_ref, normed_ref):
    rows = x_ref.shape[0]
    step = 128
    for b in range(rows // step):
        part = slice(b * step, (b + 1) * step)
        normed_ref[part, :] = normalize(x_ref[part, :].astype(F32)).astype(BF)
    base = dot(split_rows(score_ref[...]), x_ref[...], ((1,), (1,)))
    base_ref[...] = jnp.sum(base, axis=0, keepdims=True)
    fill(buf_ref, slots, first, place_ref, normed_ref)


def flip(v, scale=1.0):
    return jnp.transpose(v.astype(F32) * scale).astype(BF)


def new_kernel(
    slots, length_ref, new_ref, w_in_ref, keys_ref, values_ref, w_out_ref, score_ref, x_ref, place_ref,
    k_ref, v_ref, wq_ref, wu_ref, vec_ref, out_ref, buf_ref, base_ref, normed_ref,
):
    fill_second(slots, slots, x_ref, place_ref, score_ref, buf_ref, base_ref, normed_ref)
    length = length_ref[0]
    fresh, width = new_ref.shape
    hist = keys_ref.shape[0]
    size = width // HEADS
    step = 256
    rows = new_ref[...].astype(F32)
    normed = normalize(rows).astype(BF)
    cut = [
        silu(dot(normed, w_in_ref[:, i * width : (i + 1) * width])).astype(BF) for i in range(4)
    ]
    gate, value, query, key = cut
    k_ref[0:hist, :] = keys_ref[...]
    k_ref[hist : hist + fresh, :] = key
    for i in range(0, hist, step):
        kept = lax.broadcasted_iota(jnp.int32, (step, step), 0) + i < length
        for j in range(0, width, step):
            block = values_ref[i : i + step, j : j + step].astype(F32)
            v_ref[j : j + step, i : i + step] = flip(jnp.where(kept, block, 0.0))
    v_ref[:, hist : hist + fresh] = flip(value)
    for i in range(0, width, step):
        for j in range(0, width, step):
            wu_ref[j : j + step, i : i + step] = flip(w_in_ref[i : i + step, j : j + step], 0.5)
            wq_ref[j : j + step, i : i + step] = flip(
                w_in_ref[i : i + step, 2 * width + j : 2 * width + j + step], 0.5
            )
    vec = jnp.sum(dot(split_rows(score_ref[...]), w_out_ref[...], ((1,), (1,))), axis=0, keepdims=True)
    vec_ref[...] = split_rows(vec)
    total = hist + fresh
    at = lax.broadcasted_iota(jnp.int32, (fresh, total), 1)
    line = lax.broadcasted_iota(jnp.int32, (fresh, total), 0)
    keep = at <= line + hist
    outs = []
    for h in range(HEADS):
        cols = slice(h * size, (h + 1) * size)
        s = dot(query[:, cols], k_ref[:, cols], ((1,), (1,))) * (1.0 / size**0.5)
        a = jnp.where(keep, silu(s), 0.0).astype(BF)
        outs.append(dot(a, v_ref[cols, :], ((1,), (1,))))
    number = lax.broadcasted_iota(jnp.int32, (fresh, 1), 0) + (length + 1)
    att = (jnp.concatenate(outs, axis=1) / number.astype(F32)).astype(BF)
    gated = (normalize(att.astype(F32)) * gate.astype(F32)).astype(BF)
    out_ref[...] = (rows + dot(gated, w_out_ref[...])).astype(BF)


def rank_lines(share, x, wq, wu, k, v, vec, need):
    width = x.shape[1]
    size = width // HEADS
    step = 256

    def act(half):
        return half + half * jnp.tanh(half)

    def project(w, scale):
        parts = [dot(w[i : i + step, :], x, ((1,), (1,))) for i in range(0, width, step)]
        return jnp.concatenate([(act(p) * scale).astype(BF) for p in parts], axis=0)

    need("wq")
    query = project(wq, 0.5 / size**0.5)
    outs = []
    need("k")
    for h in range(HEADS):
        cols = slice(h * size, (h + 1) * size)
        a = act(dot(k[:, cols], query[cols, :])).astype(BF)
        need("v")
        outs.append((dot(v[cols, :], a) * share).astype(BF))
    att = jnp.concatenate(outs, axis=0).astype(F32)
    need("wu")
    gate = project(wu, 1.0)
    mean = jnp.mean(att, axis=0, keepdims=True)
    cent = att - mean
    var = jnp.mean(cent * cent, axis=0, keepdims=True)
    gated = (cent * lax.rsqrt(var + 1e-06) * gate.astype(F32)).astype(BF)
    return jnp.sum(dot(vec[...], gated), axis=0, keepdims=True)


def rank_kernel(last, *refs):
    if last:
        length_ref, vec_ref, prev_ref, x_hbm, wq_hbm, wu_hbm, k_hbm, v_hbm, out_ref = refs[:9]
    else:
        length_ref, vec_ref, x_hbm, wq_hbm, wu_hbm, k_hbm, v_hbm, out_ref = refs[:8]
    x, wq, wu, k, v, sem = refs[-6:]
    cuts = [slice(i, i + TILE) for i in range(0, x.shape[0], TILE)]
    loads = [("x0", x_hbm.at[cuts[0], :], x.at[cuts[0], :]), ("wq", wq_hbm, wq)]
    loads += [("k", k_hbm, k), ("v", v_hbm, v), ("wu", wu_hbm, wu)]
    loads += [(f"x{i}", x_hbm.at[c, :], x.at[c, :]) for i, c in enumerate(cuts) if i > 0]
    moves = {}
    for i, (name, a, b) in enumerate(loads):
        moves[name] = pltpu.make_async_copy(a, b, sem.at[i])
        moves[name].start()
    share = 1.0 / (length_ref[0] + NEW).astype(F32)
    line_ref = refs[-7]

    @pl.loop(0, len(cuts))
    def _(i):
        met = set()

        def need(name, at=0):
            if name not in met:
                met.add(name)
                pl.when(i == at)(moves[name].wait)

        for n in range(len(cuts)):
            need(f"x{n}", n)
        rows = x[pl.ds(pl.multiple_of(i * TILE, TILE), TILE), :]
        if not last:
            rows = normalize(rows.astype(F32)).astype(BF)
        line_ref[pl.ds(i, 1), :] = rank_lines(share, rows, wq, wu, k, v, vec_ref, need)

    odd = lax.rem(lax.broadcasted_iota(jnp.int32, (16, 128), 0), 2) == 1
    for i, c in enumerate(cuts):
        line = line_ref[i : i + 1, :]
        if not last:
            out_ref[:, c] = line
            continue
        for j in range(TILE // 128):
            b = i * (TILE // 128) + j
            mine = line[:, j * 128 : (j + 1) * 128]
            early = prev_ref[:, b * 128 : (b + 1) * 128]
            out_ref[16 * b : 16 * (b + 1), :] = jnp.where(odd, mine, early)


def score_kernel(me_ref, place_ref, base_ref, ret_ref, out_ref):
    parties = ret_ref.shape[0] // 2
    rows = base_ref.shape[1]
    owner = place_ref[0:1, :]
    position = place_ref[1:2, :]
    half = position >= SLOTS
    at = 2 * owner + half.astype(jnp.int32)
    match = lax.broadcasted_iota(jnp.int32, (2 * parties, rows), 0) == at
    match = jnp.where(match, 1.0, 0.0).astype(BF)
    got = jnp.zeros((128, rows), F32)
    for part in split3(ret_ref[...]):
        got += dot(part, match, ((0,), (0,)))
    lane = position - jnp.where(half, SLOTS, 0) + lax.rem(me_ref[0], 128 // SLOTS) * SLOTS
    slot = lax.broadcasted_iota(jnp.int32, (128, rows), 0) == lane
    out_ref[...] = base_ref[...] + jnp.sum(jnp.where(slot, got, 0.0), axis=0, keepdims=True)


def whole(n):
    return [pl.BlockSpec(memory_space=pltpu.VMEM)] * n


def far(n):
    return [pl.BlockSpec(memory_space=pl.ANY)] * n


def small(n):
    return [pl.BlockSpec(memory_space=pltpu.SMEM)] * n


def params(limit=VMEM_LIMIT):
    return pltpu.CompilerParams(vmem_limit_bytes=limit)


def cost(macs, moved, transcendentals=0):
    return pl.CostEstimate(flops=2 * macs, bytes_accessed=moved, transcendentals=transcendentals)


def on_device(
    row_x, row_user, user_owner, hist_len, new_rows, cache_keys, cache_values, w_in, w_out, w_score
):
    n_own = lax.axis_size("own")
    rows, width = row_x.shape
    users = user_owner.shape[0]
    hist = cache_keys.shape[1]
    total = hist + NEW
    count = n_own * SLOTS
    score_row = w_score.reshape(1, width)
    sds = jax.ShapeDtypeStruct
    dma = pltpu.SemaphoreType.DMA

    def all_to_all(v):
        return lax.all_to_all(v, "own", split_axis=0, concat_axis=0, tiled=True)

    buf, place = pl.pallas_call(
        lambda *refs: route_kernel(SLOTS, *refs),
        out_shape=(sds((count, width), BF), sds((2, rows), jnp.int32)),
        in_specs=whole(3),
        out_specs=tuple(whole(2)),
        compiler_params=params(),
        cost_estimate=cost(rows * width * count, 2 * 2 * rows * width),
        name="route",
    )(row_x, row_user.reshape(1, rows), user_owner.reshape(1, users))
    piece0 = all_to_all(buf.reshape(n_own, SLOTS, width)).reshape(count, width)

    keys, values, wq, wu, vec, new_out, buf, base = pl.pallas_call(
        lambda *refs: new_kernel(SLOTS, *refs),
        out_shape=(
            sds((total, width), BF),
            sds((width, total), BF),
            sds((width, width), BF),
            sds((width, width), BF),
            sds((8, width), BF),
            sds((NEW, width), BF),
            sds((count, width), BF),
            sds((1, rows), F32),
        ),
        in_specs=small(1) + whole(8),
        out_specs=tuple(whole(8)),
        scratch_shapes=[pltpu.VMEM((rows, width), BF)],
        compiler_params=params(),
        cost_estimate=cost(8 * NEW * width * width + rows * width * count, 24 * width * width),
        name="fresh",
    )(hist_len, new_rows[0], w_in, cache_keys[0], cache_values[0], w_out, score_row, row_x, place)
    piece1 = all_to_all(buf.reshape(n_own, SLOTS, width)).reshape(count, width)

    def rank(piece, prev):
        last = prev is not None
        return pl.pallas_call(
            lambda *refs: rank_kernel(last, *refs),
            out_shape=sds((2 * n_own, 128), F32) if last else sds((1, count), F32),
            in_specs=small(1) + whole(2 if last else 1) + far(5),
            out_specs=whole(1)[0],
            scratch_shapes=[
                pltpu.VMEM((count // TILE, TILE), F32),
                pltpu.VMEM((count, width), BF),
                pltpu.VMEM((width, width), BF),
                pltpu.VMEM((width, width), BF),
                pltpu.VMEM((total, width), BF),
                pltpu.VMEM((width, total), BF),
                dma((4 + count // TILE,)),
            ],
            compiler_params=params(),
            cost_estimate=cost(
                count * width * (2 * width + 4 * total), 10 * width * width, count * HEADS * total
            ),
            name="rank",
        )(hist_len, vec, *([prev] if last else []), piece, wq, wu, keys, values)

    result = rank(piece1, rank(piece0, None))
    returned = all_to_all(result.reshape(n_own, 2, 128)).reshape(2 * n_own, 128)
    scores = pl.pallas_call(
        score_kernel,
        out_shape=sds((1, rows), F32),
        in_specs=small(1) + whole(3),
        out_specs=whole(1)[0],
        compiler_params=params(8 * 1024 * 1024),
        name="scores",
    )(lax.axis_index("own").reshape(1), place, base, returned)
    return (scores.reshape(rows), new_out[None])


def solution(mesh):
    placed = (
        P(("grp", "own"), None),
        P(("grp", "own"), None),
        P("grp"),
        P(("grp", "own")),
        P(("grp", "own"), None, None),
        P(("grp", "own"), None, None),
        P(("grp", "own"), None, None),
        P(),
        P(),
        P(),
    )
    return jax.shard_map(
        on_device,
        mesh=mesh,
        in_specs=placed,
        out_specs=(P(("grp", "own")), P(("grp", "own"), None, None)),
        check_vma=False,
    )
```

profile of v0, /device:TPU:0, one launch (start us, length us, event | category | flops | bytes accessed | tf_op | source)
XLA Modules:
  0.0 116.5 jit_solution(13206943257846997301)
XLA Ops:
  0.6 5.5 %route.1 = (bf16[1024,1024]{1,0:T(8,128)(2,1)}, s32[2,1024]{1,0:T(2,128)}) custom-call(bf16[1024,1024]{1,0:T(8,128)(2,1)} %refs_7_.1, s32[1,1024]{1,0:T(1,128)} %bitcast.26, s32[1,64]{1,0:T(1,128)} %bitcast.27), custom_call_target="tpu_custom_call" | custom-call | flops 2147483648 | bytes 4194304 | tf_op jit(solution)/shard_map/route/pallas_call | solution.py:289
  6.1 11.5 %all-to-all-start = ((bf16[64,16,1024]{2,1,0:T(8,128)(2,1)}), bf16[64,16,1024]{2,1,0:T(8,128)(2,1)S(1)}, u32[]{:S(2)}, u32[]{:S(2)}) async-start(bf16[64,16,1024]{2,1,0:T(8,128)(2,1)} %bitcast.20), calls=%async_computation | async-start | bytes 4194304 | tf_op jit(solution)/shard_map/all_to_all | solution.py:287
  18.3 17.1 %fresh.1 = (bf16[1088,1024]{1,0:T(8,128)(2,1)}, bf16[1024,1088]{1,0:T(8,128)(2,1)}, bf16[1024,1024]{1,0:T(8,128)(2,1)}, bf16[1024,1024]{1,0:T(8,128)(2,1)}, bf16...) custom-call(s32[1]{0:T(128)S(6)} %copy.12.refs_0_, ...), custom_call_target="tpu_custom_call" | custom-call | flops 3221225472 | bytes 25165824 | tf_op jit(solution)/shard_map/fresh/pallas_call | solution.py:300
  35.4 12.7 %all-to-all-done = bf16[64,16,1024]{2,1,0:T(8,128)(2,1)S(1)} async-done(((bf16[64,16,1024]{2,1,0:T(8,128)(2,1)}), bf16[64,16,1024]{2,1,0:T(8,128)(2,1)S(1)}, u32[]{:S(2)}, u32[]{:S(2)}) %all-to-all-start) | async-done | bytes 2097184 | tf_op jit(solution)/shard_map/all_to_all | solution.py:287
  48.1 0.0 copy-start.2
  48.1 1.3 %copy-done.2 = bf16[64,16,1024]{2,1,0:T(8,128)(2,1)} copy-done((bf16[64,16,1024]{2,1,0:T(8,128)(2,1)}, bf16[64,16,1024]{2,1,0:T(8,128)(2,1)S(1)}, u32[]{:S(2)}) %copy-start.2) | copy-done | bytes 2097176
  49.4 5.8 %all-to-all-start.1 = ((bf16[64,16,1024]{2,1,0:T(8,128)(2,1)}), bf16[64,16,1024]{2,1,0:T(8,128)(2,1)}, u32[]{:S(2)}, u32[]{:S(2)}) async-start(bf16[64,16,1024]{2,1,0:T(8,128)(2,1)} %bitcast.19), calls=%async_computation.1 | async-start | bytes 4194304 | tf_op jit(solution)/shard_map/all_to_all | solution.py:287
  55.2 17.9 %rank.2.refs_2_ = f32[1,1024]{1,0:T(1,128)} custom-call(s32[1]{0:T(128)S(6)} %copy.12.refs_0_, bf16[8,1024]{1,0:T(8,128)(2,1)} %get-tuple-element.14.refs_1_, bf16[1024,1024]{1,0:T(8,128)(2,1)} %bitcast.18, bf16[1024,1024]{1,0:T(8,128)(2,1)} %get-tuple-element.16.refs_3_.refs_4_, bf16[1024,1024]{1,0:T(8,128)(2,1)} %get-tuple-element.17.refs_4_.refs_5_, ...), custom_call_target="tpu_custom_call" | custom-call | flops 13421772800 | bytes 10485760 | tf_op jit(solution)/shard_map/rank/pallas_call | solution.py:323
  73.1 10.6 %all-to-all-done.1 = bf16[64,16,1024]{2,1,0:T(8,128)(2,1)} async-done(((bf16[64,16,1024]{2,1,0:T(8,128)(2,1)}), bf16[64,16,1024]{2,1,0:T(8,128)(2,1)}, u32[]{:S(2)}, u32[]{:S(2)}) %all-to-all-start.1) | async-done | bytes 2097184 | tf_op jit(solution)/shard_map/all_to_all | solution.py:287
  83.7 0.0 copy-start
  83.7 0.0 copy-start.1
  83.7 17.5 %rank.3 = f32[128,128]{1,0:T(8,128)} custom-call(s32[1]{0:T(128)S(6)} %copy.12.refs_0_, bf16[8,1024]{1,0:T(8,128)(2,1)} %get-tuple-element.14.refs_1_, f32[1,1024]{1,0:T(1,128)} %rank.2.refs_2_, bf16[1024,1024]{1,0:T(8,128)(2,1)} %bitcast.10.refs_3_, bf16[1024,1024]{1,0:T(8,128)(2,1)} %get-tuple-element.16.refs_3_.refs_4_, ...), custom_call_target="tpu_custom_call" | custom-call | flops 13421772800 | bytes 10485760 | tf_op jit(solution)/shard_map/rank/pallas_call | solution.py:323
  101.2 4.7 %all-to-all-start.2 = ((f32[64,2,128]{2,1,0:T(2,128)}), f32[64,2,128]{2,1,0:T(2,128)S(1)}, u32[]{:S(2)}, u32[]{:S(2)}) async-start(f32[64,2,128]{2,1,0:T(2,128)} %bitcast.22), calls=%async_computation.2 | async-start | bytes 131072 | tf_op jit(solution)/shard_map/all_to_all | solution.py:287
  105.9 9.6 %all-to-all-done.2 = f32[64,2,128]{2,1,0:T(2,128)S(1)} async-done(((f32[64,2,128]{2,1,0:T(2,128)}), f32[64,2,128]{2,1,0:T(2,128)S(1)}, u32[]{:S(2)}, u32[]{:S(2)}) %all-to-all-start.2) | async-done | bytes 65568 | tf_op jit(solution)/shard_map/all_to_all | solution.py:287
  115.5 0.0 copy-done
  115.5 0.0 copy-done.1
  115.5 1.0 scores.1
Async XLA Ops:
  6.1 42.0 %all-to-all-start = ((bf16[64,16,1024]{2,1,0:T(8,128)(2,1)}), bf16[64,16,1024]{2,1,0:T(8,128)(2,1)S(1)}, u32[]{:S(2)}, u32[]{:S(2)}) async-start(bf16[64,16,1024]{2,1,0:T(8,128)(2,1)} %bitcast.20), calls=%async_computation | async-start | bytes 4194304 | tf_op jit(solution)/shard_map/all_to_all | solution.py:287
  48.1 1.3 %copy-start.2 = (bf16[64,16,1024]{2,1,0:T(8,128)(2,1)}, bf16[64,16,1024]{2,1,0:T(8,128)(2,1)S(1)}, u32[]{:S(2)}) copy-start(bf16[64,16,1024]{2,1,0:T(8,128)(2,1)S(1)} %all-to-all-done) | copy-start | bytes 6291460
  49.4 34.3 %all-to-all-start.1 = ((bf16[64,16,1024]{2,1,0:T(8,128)(2,1)}), bf16[64,16,1024]{2,1,0:T(8,128)(2,1)}, u32[]{:S(2)}, u32[]{:S(2)}) async-start(bf16[64,16,1024]{2,1,0:T(8,128)(2,1)} %bitcast.19), calls=%async_computation.1 | async-start | bytes 4194304 | tf_op jit(solution)/shard_map/all_to_all | solution.py:287
  83.7 31.8 %copy-start = (s32[2,1024]{1,0:T(2,128)S(1)}, s32[2,1024]{1,0:T(2,128)}, u32[]{:S(2)}) copy-start(s32[2,1024]{1,0:T(2,128)} %get-tuple-element.12.refs_8_.place_ref) | copy-start | bytes 24580
  83.7 31.8 %copy-start.1 = (f32[1,1024]{1,0:T(1,128)S(1)}, f32[1,1024]{1,0:T(1,128)}, u32[]{:S(2)}) copy-start(f32[1,1024]{1,0:T(1,128)} %get-tuple-element.13.base_ref) | copy-start | bytes 12292
  101.2 14.3 %all-to-all-start.2 = ((f32[64,2,128]{2,1,0:T(2,128)}), f32[64,2,128]{2,1,0:T(2,128)S(1)}, u32[]{:S(2)}, u32[]{:S(2)}) async-start(f32[64,2,128]{2,1,0:T(2,128)} %bitcast.22), calls=%async_computation.2 | async-start | bytes 131072 | tf_op jit(solution)/shard_map/all_to_all | solution.py:287
where the time goes:
time: 117 us
  Pallas kernels  59 us (50%)
  waiting for transfers between devices  32.9 us (28%)
  starting transfers between devices  21.9 us (19%)
  between operations  1.33 us (1%)
  local copies, waits for them, and re-layouts  1.32 us (1%)
    pallas_call x2, Pallas kernels, rank(): pl.pallas_call(lambda *refs: rank_kernel(last, *refs), out_shape=sds((2 *...  35.3 us
    all_to_all x3, waiting for transfers between devices, all_to_all(): return lax.all_to_all(v, 'own', split_axis=0, concat_axis=0, tiled=True)  32.9 us
    all_to_all x3, starting transfers between devices, all_to_all(): return lax.all_to_all(v, 'own', split_axis=0, concat_axis=0, tiled=True)  21.9 us
    pallas_call x1, Pallas kernels, on_device(): pl.pallas_call(lambda *refs: new_kernel(SLOTS, *refs), out_shape=(sds((to...  17.1 us
    pallas_call x1, Pallas kernels, on_device(): pl.pallas_call(lambda *refs: route_kernel(SLOTS, *refs), out_shape=(sds((...  5.51 us
  transfers between devices with their start and end apart: 3, of which 3 were waited for; matrix products, arithmetic and copies ran while one was open for 0% of the time, Pallas kernels for 30%

commit v1 on v0

--- a/solution.py
+++ b/solution.py
@@ -79,10 +79,10 @@
     position = place_ref[1:2, :]
     inside = jnp.logical_and(position >= first, position < first + slots)
     key = jnp.where(inside, owner * slots + position - first, -1)
-    step = 256
+    step = 512
+    at = lax.broadcasted_iota(jnp.int32, (step, rows), 0)
     for b in range(out_ref.shape[0] // step):
-        at = lax.broadcasted_iota(jnp.int32, (step, rows), 0) + b * step
-        pick = jnp.where(at == key, 1.0, 0.0).astype(BF)
+        pick = jnp.where(at == key - b * step, 1.0, 0.0).astype(BF)
         out_ref[b * step : (b + 1) * step, :] = dot(pick, normed_ref[...]).astype(BF)
         if done is not None:
             done(b, slice(b * step, (b + 1) * step))

time: 117 us -> 117 us (level)
  no operation moved by 1% of the time
where the time goes in v1:
time: 117 us; the launch traced here: 116 us
  Pallas kernels  59 us (50%)
  waiting for transfers between devices  32.9 us (28%)
  starting transfers between devices  22 us (19%)
  between operations  1.33 us (1%)
  local copies, waits for them, and re-layouts  1.32 us (1%)
    pallas_call x2, Pallas kernels, rank(): pl.pallas_call(lambda *refs: rank_kernel(last, *refs), out_shape=sds((2 *...  35.3 us
    all_to_all x3, waiting for transfers between devices, all_to_all(): return lax.all_to_all(v, 'own', split_axis=0, concat_axis=0, tiled=True)  32.9 us
    all_to_all x3, starting transfers between devices, all_to_all(): return lax.all_to_all(v, 'own', split_axis=0, concat_axis=0, tiled=True)  22 us
    pallas_call x1, Pallas kernels, on_device(): pl.pallas_call(lambda *refs: new_kernel(SLOTS, *refs), out_shape=(sds((to...  17.1 us
    pallas_call x1, Pallas kernels, on_device(): pl.pallas_call(lambda *refs: route_kernel(SLOTS, *refs), out_shape=(sds((...  5.51 us
  transfers between devices with their start and end apart: 3, of which 3 were waited for; matrix products, arithmetic and copies ran while one was open for 0% of the time, Pallas kernels for 30%

profile of v1, /device:TPU:0, one launch (start us, length us, event | category | flops | bytes accessed | tf_op | source)
XLA Modules:
  0.0 116.5 jit_solution(11780602640046854550)
XLA Ops:
  0.6 5.5 %route.1 = (bf16[1024,1024]{1,0:T(8,128)(2,1)}, s32[2,1024]{1,0:T(2,128)}) custom-call(bf16[1024,1024]{1,0:T(8,128)(2,1)} %refs_7_.1, s32[1,1024]{1,0:T(1,128)} %bitcast.26, s32[1,64]{1,0:T(1,128)} %bitcast.27), custom_call_target="tpu_custom_call" | custom-call | flops 2147483648 | bytes 4194304 | tf_op jit(solution)/shard_map/route/pallas_call | solution.py:289
  6.1 11.5 %all-to-all-start = ((bf16[64,16,1024]{2,1,0:T(8,128)(2,1)}), bf16[64,16,1024]{2,1,0:T(8,128)(2,1)S(1)}, u32[]{:S(2)}, u32[]{:S(2)}) async-start(bf16[64,16,1024]{2,1,0:T(8,128)(2,1)} %bitcast.20), calls=%async_computation | async-start | bytes 4194304 | tf_op jit(solution)/shard_map/all_to_all | solution.py:287
  18.3 17.1 %fresh.1 = (bf16[1088,1024]{1,0:T(8,128)(2,1)}, bf16[1024,1088]{1,0:T(8,128)(2,1)}, bf16[1024,1024]{1,0:T(8,128)(2,1)}, bf16[1024,1024]{1,0:T(8,128)(2,1)}, bf16...) custom-call(s32[1]{0:T(128)S(6)} %copy.12.refs_0_, ...), custom_call_target="tpu_custom_call" | custom-call | flops 3221225472 | bytes 25165824 | tf_op jit(solution)/shard_map/fresh/pallas_call | solution.py:300
  35.4 12.7 %all-to-all-done = bf16[64,16,1024]{2,1,0:T(8,128)(2,1)S(1)} async-done(((bf16[64,16,1024]{2,1,0:T(8,128)(2,1)}), bf16[64,16,1024]{2,1,0:T(8,128)(2,1)S(1)}, u32[]{:S(2)}, u32[]{:S(2)}) %all-to-all-start) | async-done | bytes 2097184 | tf_op jit(solution)/shard_map/all_to_all | solution.py:287
  48.1 0.0 copy-start.2
  48.1 1.3 %copy-done.2 = bf16[64,16,1024]{2,1,0:T(8,128)(2,1)} copy-done((bf16[64,16,1024]{2,1,0:T(8,128)(2,1)}, bf16[64,16,1024]{2,1,0:T(8,128)(2,1)S(1)}, u32[]{:S(2)}) %copy-start.2) | copy-done | bytes 2097176
  49.4 5.8 %all-to-all-start.1 = ((bf16[64,16,1024]{2,1,0:T(8,128)(2,1)}), bf16[64,16,1024]{2,1,0:T(8,128)(2,1)}, u32[]{:S(2)}, u32[]{:S(2)}) async-start(bf16[64,16,1024]{2,1,0:T(8,128)(2,1)} %bitcast.19), calls=%async_computation.1 | async-start | bytes 4194304 | tf_op jit(solution)/shard_map/all_to_all | solution.py:287
  55.2 17.9 %rank.2.refs_2_ = f32[1,1024]{1,0:T(1,128)} custom-call(s32[1]{0:T(128)S(6)} %copy.12.refs_0_, bf16[8,1024]{1,0:T(8,128)(2,1)} %get-tuple-element.14.refs_1_, bf16[1024,1024]{1,0:T(8,128)(2,1)} %bitcast.18, bf16[1024,1024]{1,0:T(8,128)(2,1)} %get-tuple-element.16.refs_3_.refs_4_, bf16[1024,1024]{1,0:T(8,128)(2,1)} %get-tuple-element.17.refs_4_.refs_5_, ...), custom_call_target="tpu_custom_call" | custom-call | flops 13421772800 | bytes 10485760 | tf_op jit(solution)/shard_map/rank/pallas_call | solution.py:323
  73.1 10.6 %all-to-all-done.1 = bf16[64,16,1024]{2,1,0:T(8,128)(2,1)} async-done(((bf16[64,16,1024]{2,1,0:T(8,128)(2,1)}), bf16[64,16,1024]{2,1,0:T(8,128)(2,1)}, u32[]{:S(2)}, u32[]{:S(2)}) %all-to-all-start.1) | async-done | bytes 2097184 | tf_op jit(solution)/shard_map/all_to_all | solution.py:287
  83.7 0.0 copy-start
  83.7 0.0 copy-start.1
  83.7 17.5 %rank.3 = f32[128,128]{1,0:T(8,128)} custom-call(s32[1]{0:T(128)S(6)} %copy.12.refs_0_, bf16[8,1024]{1,0:T(8,128)(2,1)} %get-tuple-element.14.refs_1_, f32[1,1024]{1,0:T(1,128)} %rank.2.refs_2_, bf16[1024,1024]{1,0:T(8,128)(2,1)} %bitcast.10.refs_3_, bf16[1024,1024]{1,0:T(8,128)(2,1)} %get-tuple-element.16.refs_3_.refs_4_, ...), custom_call_target="tpu_custom_call" | custom-call | flops 13421772800 | bytes 10485760 | tf_op jit(solution)/shard_map/rank/pallas_call | solution.py:323
  101.2 4.7 %all-to-all-start.2 = ((f32[64,2,128]{2,1,0:T(2,128)}), f32[64,2,128]{2,1,0:T(2,128)S(1)}, u32[]{:S(2)}, u32[]{:S(2)}) async-start(f32[64,2,128]{2,1,0:T(2,128)} %bitcast.22), calls=%async_computation.2 | async-start | bytes 131072 | tf_op jit(solution)/shard_map/all_to_all | solution.py:287
  105.9 9.6 %all-to-all-done.2 = f32[64,2,128]{2,1,0:T(2,128)S(1)} async-done(((f32[64,2,128]{2,1,0:T(2,128)}), f32[64,2,128]{2,1,0:T(2,128)S(1)}, u32[]{:S(2)}, u32[]{:S(2)}) %all-to-all-start.2) | async-done | bytes 65568 | tf_op jit(solution)/shard_map/all_to_all | solution.py:287
  115.5 0.0 copy-done
  115.5 0.0 copy-done.1
  115.5 1.0 scores.1
Async XLA Ops:
  6.1 42.0 %all-to-all-start = ((bf16[64,16,1024]{2,1,0:T(8,128)(2,1)}), bf16[64,16,1024]{2,1,0:T(8,128)(2,1)S(1)}, u32[]{:S(2)}, u32[]{:S(2)}) async-start(bf16[64,16,1024]{2,1,0:T(8,128)(2,1)} %bitcast.20), calls=%async_computation | async-start | bytes 4194304 | tf_op jit(solution)/shard_map/all_to_all | solution.py:287
  48.1 1.3 %copy-start.2 = (bf16[64,16,1024]{2,1,0:T(8,128)(2,1)}, bf16[64,16,1024]{2,1,0:T(8,128)(2,1)S(1)}, u32[]{:S(2)}) copy-start(bf16[64,16,1024]{2,1,0:T(8,128)(2,1)S(1)} %all-to-all-done) | copy-start | bytes 6291460
  49.4 34.3 %all-to-all-start.1 = ((bf16[64,16,1024]{2,1,0:T(8,128)(2,1)}), bf16[64,16,1024]{2,1,0:T(8,128)(2,1)}, u32[]{:S(2)}, u32[]{:S(2)}) async-start(bf16[64,16,1024]{2,1,0:T(8,128)(2,1)} %bitcast.19), calls=%async_computation.1 | async-start | bytes 4194304 | tf_op jit(solution)/shard_map/all_to_all | solution.py:287
  83.7 31.8 %copy-start = (s32[2,1024]{1,0:T(2,128)S(1)}, s32[2,1024]{1,0:T(2,128)}, u32[]{:S(2)}) copy-start(s32[2,1024]{1,0:T(2,128)} %get-tuple-element.12.refs_8_.place_ref) | copy-start | bytes 24580
  83.7 31.8 %copy-start.1 = (f32[1,1024]{1,0:T(1,128)S(1)}, f32[1,1024]{1,0:T(1,128)}, u32[]{:S(2)}) copy-start(f32[1,1024]{1,0:T(1,128)} %get-tuple-element.13.base_ref) | copy-start | bytes 12292
  101.2 14.3 %all-to-all-start.2 = ((f32[64,2,128]{2,1,0:T(2,128)}), f32[64,2,128]{2,1,0:T(2,128)S(1)}, u32[]{:S(2)}, u32[]{:S(2)}) async-start(f32[64,2,128]{2,1,0:T(2,128)} %bitcast.22), calls=%async_computation.2 | async-start | bytes 131072 | tf_op jit(solution)/shard_map/all_to_all | solution.py:287
